TPU v7x, 128 devices: a whole 4x4x4 slice. The times are simulated.
128 devices in a mesh: ctx: 32 (over x, z, core), tp: 4 (over y).
Axes of the slice: x: 4, y: 4, z: 4, core: 2. Of those that a mesh axis runs over, the one named last changes fastest.
Arguments:
- q_in: bfloat16 [8192, 8192], P('ctx', 'tp'), may hold values from -60 to 60
- k_in: bfloat16 [8192, 1024], P('ctx', 'tp'), may hold values from -6 to 6
- v_in: bfloat16 [8192, 1024], P('ctx', 'tp'), may hold values from -6 to 6
- doc_ids: int32 [8192], replicated, may hold values from 0 to 127, never falling along the last dimension, each value on 1 to 1024 neighbouring positions
- x_in: bfloat16 [8192, 16384], P('ctx', 'tp'), may hold values from -6 to 6
- b_in: bfloat16 [8192, 1024], P('ctx', 'tp'), may hold values from -6 to 6
- c_in: bfloat16 [8192, 1024], P('ctx', 'tp'), may hold values from -6 to 6
- z_gate: bfloat16 [8192, 16384], P('ctx', 'tp'), may hold values from -6 to 6
- dt_raw: bfloat16 [8192, 256], P('ctx', 'tp'), may hold values from -5 to 5
- conv_x: bfloat16 [4, 16384], P(None, 'tp'), may hold values from -3 to 3
- conv_b: bfloat16 [4, 1024], P(None, 'tp'), may hold values from -3 to 3
- conv_c: bfloat16 [4, 1024], P(None, 'tp'), may hold values from -3 to 3
- dt_bias: float32 [256], P('tp'), may hold values from -2 to 1
- rates: float32 [256], P('tp'), may hold values from 0.0002 to 0.05
- skip_d: float32 [256], P('tp'), may hold values from 0.5 to 1.5
- norm_gain: float32 [16384], P('tp'), may hold values from 0.5 to 1.5
Outputs:
- attn_out: bfloat16 [8192, 8192], P('ctx', 'tp')
- mamba_out: bfloat16 [8192, 16384], P('ctx', 'tp')
Inputs may be any that keep to these rules, and one draw needn't show every extreme that they name: `doc_ids`: document ids never fall along the pack; a document covers 1 to 1024 tokens and one covers exactly 1024.
All inputs are finite; a program needn't handle non-finite values.
Results may differ from a plain program's by a relative error of at most 0.0065.
Values may be sent and summed in bfloat16 or wider, within the bound.
A program may use at most 192 MiB of HBM per device.

v0:
```python
import functools

import jax
import jax.numpy as jnp
from jax import lax
from jax.experimental import pallas as pl
from jax.experimental.pallas import tpu as pltpu
from jax.sharding import PartitionSpec as P

HEAD_DIM = 128
STATE = 128
INNER = 16384
EPSILON = 1e-05
FAR = 1e30
LOG2E = 1.4426950408889634

TOK = 256
WIDE = 512
MESH = pl.DeviceIdType.MESH
F32 = jnp.float32
BF16 = jnp.bfloat16

RIM_X, RIM_B, RIM_C, K1, V1, K2, V2, KX, VX, K1S, V1S, E_SIB, T_SIB, E_C1, E_C2, T_C, IN_SIB, SQ = range(18)
COPIES = SQ + 3
L_X, L_Z, L_Q, L_K, L_V, L_B, L_C, L_AO, L_MO = range(9)


def dot(a, b):
    return lax.dot_general(a, b, (((1,), (0,)), ((), ())), preferred_element_type=F32)


def dot_nt(a, b):
    return lax.dot_general(a, b, (((1,), (1,)), ((), ())), preferred_element_type=F32)


def silu(a):
    half = 0.5 * a
    return half + half * jnp.tanh(half)


def repeat_lanes(a, times):
    return jnp.concatenate([a] * times, axis=1)


def split2(a):
    high = a.astype(BF16).astype(F32)
    return jnp.concatenate([high, a - high], axis=1).astype(BF16)


def kernel(
    n_ctx,
    n_tp,
    q_hbm,
    k_hbm,
    v_hbm,
    ids,
    x_hbm,
    b_hbm,
    c_hbm,
    z_hbm,
    dt_raw,
    conv_x,
    conv_b,
    conv_c,
    dt_bias,
    rates,
    skip_d,
    gain,
    ao_hbm,
    mo_hbm,
    xv,
    zv,
    qv,
    kbuf,
    vbuf,
    bv,
    cv,
    rim_x,
    rim_b,
    rim_c,
    g1,
    gate,
    e_own,
    e_sib,
    e_chip,
    e_n1,
    e_n2,
    in_own,
    in_sib,
    t_own,
    t_sib,
    t_chip,
    t_n1,
    sq_own,
    sq_in,
    expand,
    shift,
    mix,
    bt,
    cj,
    far_own,
    hot,
    tri_bias,
    ao,
    mo,
    sumsq,
    send,
    recv,
    local,
):
    p = lax.axis_index("ctx")
    t = lax.axis_index("tp")
    core = lax.rem(p, 2)
    sib = p + 1 - 2 * core
    channels = x_hbm.shape[1]
    groups = channels // 2048
    half_width = channels // 2

    def at(offset):
        return lax.rem(p + offset + n_ctx, n_ctx)

    def remote(src, dst, slot, to, tp=None):
        return pltpu.make_async_remote_copy(
            src_ref=src,
            dst_ref=dst,
            send_sem=send.at[slot],
            recv_sem=recv.at[slot],
            device_id=(to, t if tp is None else tp),
            device_id_type=MESH,
        )

    loads = {
        L_B: pltpu.make_async_copy(b_hbm, bv, local.at[L_B]),
        L_C: pltpu.make_async_copy(c_hbm, cv, local.at[L_C]),
        L_X: pltpu.make_async_copy(x_hbm, xv, local.at[L_X]),
        L_Z: pltpu.make_async_copy(z_hbm, zv, local.at[L_Z]),
        L_K: pltpu.make_async_copy(k_hbm, kbuf.at[0], local.at[L_K]),
        L_V: pltpu.make_async_copy(v_hbm, vbuf.at[0], local.at[L_V]),
        L_Q: pltpu.make_async_copy(q_hbm, qv, local.at[L_Q]),
    }

    barrier = pltpu.get_barrier_semaphore()
    for source in (sib, at(-1), at(-2), at(-4)):
        pl.semaphore_signal(barrier, inc=1, device_id=(source, t), device_id_type=MESH)
    for step in range(1, n_tp):
        pl.semaphore_signal(
            barrier, inc=1, device_id=(p, lax.rem(t + n_tp - step, n_tp)), device_id_type=MESH
        )
    for slot in (L_B, L_C, L_X, L_Z, L_K, L_V, L_Q):
        loads[slot].start()
    pl.semaphore_wait(barrier, 4 + n_tp - 1)

    last_rows = pl.ds(TOK - 16, 16)
    rims = [
        remote(b_hbm.at[last_rows], rim_b, RIM_B, at(1)),
        remote(c_hbm.at[last_rows], rim_c, RIM_C, at(1)),
        remote(x_hbm.at[last_rows], rim_x, RIM_X, at(1)),
    ]
    for copy in rims:
        copy.start()
    near = [
        remote(k_hbm, kbuf.at[1], K1, at(2)),
        remote(v_hbm, vbuf.at[1], V1, at(2)),
    ]
    far = [
        remote(k_hbm, kbuf.at[3], K2, at(4)),
        remote(v_hbm, vbuf.at[3], V2, at(4)),
    ]
    for copy in near + far:
        copy.start()
    own_to_sib = [
        remote(k_hbm, kbuf.at[4], KX, sib),
        remote(v_hbm, vbuf.at[4], VX, sib),
    ]

    @pl.when(core == 0)
    def _():
        for copy in own_to_sib:
            copy.start()

    def id_row(row):
        return ids[pl.ds(row, 1), :].astype(F32)

    def id_column(row):
        return jnp.broadcast_to(id_row(row), (128, 128)).T

    def id_columns(device):
        return jnp.concatenate([id_column(2 * device), id_column(2 * device + 1)], axis=0)

    own_cols = id_columns(p)
    own_row = jnp.concatenate([id_row(2 * p), id_row(2 * p + 1)], axis=1)
    last_id = own_row[:, TOK - 1 : TOK]
    before_row = lax.rem(2 * p - 1 + 2 * n_ctx, 2 * n_ctx)
    first_device = p == 0
    before_cols = jnp.where(first_device, -1.0, id_column(before_row))
    before_id = jnp.where(first_device, -1.0, id_row(before_row))[:, 127:128]
    lanes = lax.broadcasted_iota(jnp.int32, (TOK, 128), 1).astype(F32)
    far_own[...] = jnp.where(own_cols == lanes, 0.0, -FAR).astype(BF16)
    block_devices = (p, p - 2, p - 1 - 2 * core, p - 4, p - 3 + 2 * core)
    for slot, device in enumerate(block_devices):
        columns = id_columns(lax.rem(device + n_ctx, n_ctx)) if slot else own_cols
        hot[slot] = jnp.where(columns == lanes, 1.0, 0.0).astype(BF16)
    row_at = lax.broadcasted_iota(jnp.int32, (TOK, TOK), 0)
    col_at = lax.broadcasted_iota(jnp.int32, (TOK, TOK), 1)
    same = repeat_lanes(own_cols, 2) == own_row
    causal = col_at <= row_at
    allowed = same & causal
    tri_bias[...] = jnp.where(causal, 0.0, -FAR)
    for back in range(1, 4):
        shift[pl.ds((back - 1) * TOK, TOK), :] = jnp.where(
            same & (row_at - col_at == back), 1.0, 0.0
        ).astype(BF16)
    tops = lax.broadcasted_iota(jnp.int32, (8, 128), 0)
    rim_keep = [
        jnp.where(
            (tops < back) & (own_cols[:8] == pltpu.roll(before_cols[120:], back, 0)), 1.0, 0.0
        )
        for back in range(1, 4)
    ]

    raw = dt_raw[...].astype(F32) + dt_bias[...]
    steps = jnp.maximum(raw, 0.0) + jnp.log(1.0 + jnp.exp(-jnp.abs(raw)))
    log_decay = -steps * rates[...]
    upto = jnp.where(causal, 1.0, 0.0).astype(BF16)
    part = log_decay.astype(BF16)
    rest = log_decay - part.astype(F32)
    part2 = rest.astype(BF16)
    part3 = (rest - part2.astype(F32)).astype(BF16)
    cum = dot(upto, part) + (dot(upto, part2) + dot(upto, part3))
    middle = cum[TOK // 2 - 1 : TOK // 2]
    end = cum[TOK - 1 : TOK]
    expand[pl.ds(0, TOK), :] = split2(jnp.exp(middle - cum) * steps)
    expand[pl.ds(TOK, TOK), :] = split2(jnp.exp(cum - middle))
    continues = before_id == last_id
    through = jnp.where(continues, jnp.exp(end), 0.0)
    wide_through = jnp.concatenate([through, through], axis=1)
    t_own[...] = jnp.broadcast_to(wide_through, (8, 128))
    rows = lax.broadcasted_iota(jnp.int32, (16, 64), 0)
    vectors = jnp.where(rows == 0, jnp.exp(end - middle), jnp.where(rows == 1, skip_d[...], 0.0))
    expand[pl.ds(2 * TOK, 16), :] = split2(vectors)
    middle_factor = jnp.exp(middle)

    def spread_matrix(tile):
        head = lax.broadcasted_iota(jnp.int32, (128, WIDE), 0) & 63
        place = (lax.broadcasted_iota(jnp.int32, (128, WIDE), 1) >> 6) + tile * (WIDE // 64)
        return jnp.where(head == place, 1.0, 0.0).astype(BF16)

    def conv(source, rim, weights, width):
        moved = dot(shift[...], source)
        taps = weights.astype(F32)
        total = taps[3:4] * source.astype(F32)
        edge = jnp.zeros((8, width), F32)
        rim8 = rim.astype(F32)[8:16]
        for back in range(1, 4):
            tap = taps[3 - back : 4 - back]
            total = total + tap * moved[(back - 1) * TOK : back * TOK]
            keep = repeat_lanes(rim_keep[back - 1], width // 128)
            edge = edge + tap * (keep * pltpu.roll(rim8, back, 0))
        total = jnp.concatenate([total[:8] + edge, total[8:]], axis=0)
        return silu(total).astype(BF16)

    for slot in (L_B, L_C):
        loads[slot].wait()
    for copy in rims:
        copy.wait()
    b_conv = conv(bv[...], rim_b[...], conv_b[...], bv.shape[1])
    c_conv = conv(cv[...], rim_c[...], conv_c[...], cv.shape[1])
    for group in range(groups):
        b_group = b_conv[:, group * STATE : (group + 1) * STATE]
        c_group = c_conv[:, group * STATE : (group + 1) * STATE]
        mix[group] = jnp.where(allowed, dot_nt(c_group, b_group), 0.0).astype(BF16)
        ending = jnp.where(own_cols == last_id, b_group.astype(F32), 0.0)
        bt[group] = ending.T.astype(BF16)
        cj[group] = jnp.where(own_cols == before_id, c_group.astype(F32), 0.0).astype(BF16)

    loads[L_X].wait()
    loads[L_Z].wait()
    tiles_per_group = 2048 // WIDE

    def ssd_tile(tile, carry):
        group = tile // tiles_per_group
        here = pl.ds(pl.multiple_of(tile * WIDE, WIDE), WIDE)
        x_conv = conv(xv[:, here], rim_x[:, here], conv_x[:, here], WIDE)
        factors = dot(expand[...], spread_matrix(tile))
        x_wide = x_conv.astype(F32)
        x_scaled = (x_wide * factors[:TOK]).astype(BF16)
        inside = dot(mix[group], x_scaled)
        e_own[:, here] = (dot(bt[group], x_scaled) * factors[2 * TOK : 2 * TOK + 1]).astype(BF16)
        open_gate = silu(zv[:, here].astype(F32))
        leaving = factors[TOK : 2 * TOK]
        full = leaving * inside + factors[2 * TOK + 1 : 2 * TOK + 2] * x_wide
        g1[:, here] = full * open_gate
        gate[:, here] = leaving * open_gate
        return carry

    lax.fori_loop(0, channels // WIDE, ssd_tile, 0)

    to_sib = [remote(e_own, e_sib, E_SIB, sib), remote(t_own, t_sib, T_SIB, sib)]
    for copy in to_sib:
        copy.start()
    for copy in near:
        copy.wait()
    sib_near = [
        remote(kbuf.at[1], kbuf.at[2], K1S, sib),
        remote(vbuf.at[1], vbuf.at[2], V1S, sib),
    ]
    for copy in sib_near:
        copy.start()
    for copy in to_sib:
        copy.wait()

    t_chip[...] = t_own[...] * t_sib[...]
    is_low = core == 0
    u_own = split2(jnp.where(is_low, t_sib[...], 1.0)[:, :64])
    u_sib = split2(jnp.where(is_low, 1.0, t_own[...])[:, :64])
    u_both = jnp.concatenate([u_own, u_sib], axis=0)
    half_tiles = half_width // WIDE

    def chip_tile(tile, carry):
        whole = core * half_tiles + tile
        here = pl.ds(pl.multiple_of(tile * WIDE, WIDE), WIDE)
        there = pl.ds(pl.multiple_of(whole * WIDE, WIDE), WIDE)
        factors = dot(u_both, spread_matrix(whole))
        e_chip[:, here] = (
            factors[0:1] * e_own[:, there].astype(F32) + factors[8:9] * e_sib[:, there].astype(F32)
        ).astype(BF16)
        return carry

    lax.fori_loop(0, half_tiles, chip_tile, 0)
    chip_sends = [
        remote(t_chip, t_n1, T_C, at(2)),
        remote(e_chip, e_n1, E_C1, at(2)),
        remote(e_chip, e_n2, E_C2, at(4)),
    ]
    for copy in chip_sends:
        copy.start()

    for copy in far:
        copy.wait()
    far_to_sib = [
        remote(kbuf.at[3], kbuf.at[4], KX, sib),
        remote(vbuf.at[3], vbuf.at[4], VX, sib),
    ]

    @pl.when(core == 1)
    def _():
        for copy in far_to_sib:
            copy.start()
            copy.wait_send()

    @pl.when(core == 0)
    def _():
        for copy in own_to_sib:
            copy.wait_send()

    for copy in far_to_sib:
        copy.wait_recv()
    for copy in sib_near:
        copy.wait()
    for slot in (L_K, L_V, L_Q):
        loads[slot].wait()

    factor = HEAD_DIM**-0.5 * LOG2E
    query_heads = q_hbm.shape[1] // HEAD_DIM
    per_kv = query_heads // (k_hbm.shape[1] // HEAD_DIM)

    def attend(head, carry):
        here = pl.ds(pl.multiple_of(head * HEAD_DIM, HEAD_DIM), HEAD_DIM)
        kv = pl.ds(pl.multiple_of((head // per_kv) * HEAD_DIM, HEAD_DIM), HEAD_DIM)
        query = jnp.concatenate([qv[:, here], far_own[...]], axis=1)
        scores = []
        for slot in range(5):
            key = jnp.concatenate([kbuf[slot, :, kv], hot[slot]], axis=1)
            scores.append(dot_nt(query, key))
        scores[0] = scores[0] + tri_bias[...]
        top = functools.reduce(jnp.maximum, scores)
        top = jnp.max(top, axis=1, keepdims=True) * factor
        ones = jnp.ones((TOK, HEAD_DIM), BF16)
        summed = jnp.zeros((TOK, 2 * HEAD_DIM), F32)
        for slot in range(5):
            weights = jnp.exp2(scores[slot] * factor - top).astype(BF16)
            value = jnp.concatenate([vbuf[slot, :, kv], ones], axis=1)
            summed = summed + dot(weights, value)
        ao[:, here] = (summed[:, :HEAD_DIM] / summed[:, HEAD_DIM:]).astype(BF16)
        return carry

    lax.fori_loop(0, query_heads, attend, 0)
    ao_out = pltpu.make_async_copy(ao, ao_hbm, local.at[L_AO])
    ao_out.start()

    for copy in chip_sends:
        copy.wait()
    u_chip = split2(t_n1[...][:, :64])

    def in_tile(tile, carry):
        here = pl.ds(pl.multiple_of(tile * WIDE, WIDE), WIDE)
        factors = dot(u_chip, spread_matrix(core * half_tiles + tile))
        in_own[:, here] = (
            e_n1[:, here].astype(F32) + factors[0:1] * e_n2[:, here].astype(F32)
        ).astype(BF16)
        return carry

    lax.fori_loop(0, half_tiles, in_tile, 0)
    swap = remote(in_own, in_sib, IN_SIB, sib)
    swap.start()

    w_sib = split2(jnp.where(is_low, 0.0, jnp.broadcast_to(middle_factor, (8, 64))))
    w_in = split2(jnp.where(is_low, 1.0, t_sib[...])[:, :64] * middle_factor)
    w_both = jnp.concatenate([w_sib, w_in], axis=0)
    sumsq[...] = jnp.zeros_like(sumsq)

    def join_tiles(incoming, first):
        def join_tile(tile, carry):
            whole = first + tile
            group = whole // tiles_per_group
            here = pl.ds(pl.multiple_of(tile * WIDE, WIDE), WIDE)
            there = pl.ds(pl.multiple_of(whole * WIDE, WIDE), WIDE)
            factors = dot(w_both, spread_matrix(whole))
            state = factors[0:1] * e_sib[:, there].astype(F32) + factors[8:9] * incoming[
                :, here
            ].astype(F32)
            gated = g1[:, there] + gate[:, there] * dot(cj[group], state.astype(BF16))
            g1[:, there] = gated
            squares = gated * gated
            total = sumsq[...]
            for lane in range(WIDE // 128):
                total = total + squares[:, lane * 128 : (lane + 1) * 128]
            sumsq[...] = total
            return carry

        lax.fori_loop(0, half_tiles, join_tile, 0)

    join_tiles(in_own, core * half_tiles)
    swap.wait()
    join_tiles(in_sib, (1 - core) * half_tiles)

    own_sums = jnp.concatenate(
        [
            jnp.sum(sumsq[pl.ds(0, 128), :].T, axis=0, keepdims=True),
            jnp.sum(sumsq[pl.ds(128, 128), :].T, axis=0, keepdims=True),
        ],
        axis=1,
    )
    sq_own[...] = jnp.broadcast_to(own_sums, (8, TOK))
    sq_sends = [
        remote(sq_own, sq_in.at[step - 1], SQ + step - 1, p, lax.rem(t + step, n_tp))
        for step in range(1, n_tp)
    ]
    for copy in sq_sends:
        copy.start()
    for copy in sq_sends:
        copy.wait()
    total = sq_own[...]
    for step in range(1, n_tp):
        total = total + sq_in[step - 1]
    scale = lax.rsqrt(total[0:1] / INNER + EPSILON)
    scale_cols = jnp.concatenate(
        [
            jnp.broadcast_to(scale[:, :128], (128, 128)).T,
            jnp.broadcast_to(scale[:, 128:], (128, 128)).T,
        ],
        axis=0,
    )
    scale_wide = repeat_lanes(scale_cols, WIDE // 128)

    def norm_tile(tile, carry):
        here = pl.ds(pl.multiple_of(tile * WIDE, WIDE), WIDE)
        mo[:, here] = (g1[:, here] * scale_wide * gain[:, here]).astype(BF16)
        return carry

    lax.fori_loop(0, channels // WIDE, norm_tile, 0)
    mo_out = pltpu.make_async_copy(mo, mo_hbm, local.at[L_MO])
    mo_out.start()
    ao_out.wait()
    mo_out.wait()


def per_device(q, k, v, ids, x, b, c, z, dt_raw, conv_x, conv_b, conv_c, dt_bias, rates, skip_d, gain):
    n_ctx, n_tp = lax.axis_size("ctx"), lax.axis_size("tp")
    channels = x.shape[1]
    half = channels // 2
    groups = b.shape[1] // STATE
    hbm = pl.BlockSpec(memory_space=pl.ANY)
    vmem = pl.BlockSpec(memory_space=pltpu.VMEM)
    specs = [hbm, hbm, hbm, vmem, hbm, hbm, hbm, hbm] + [vmem] * 8
    scratch = [
        pltpu.VMEM(x.shape, BF16),
        pltpu.VMEM(z.shape, BF16),
        pltpu.VMEM(q.shape, BF16),
        pltpu.VMEM((5,) + k.shape, BF16),
        pltpu.VMEM((5,) + v.shape, BF16),
        pltpu.VMEM(b.shape, BF16),
        pltpu.VMEM(c.shape, BF16),
        pltpu.VMEM((16, channels), BF16),
        pltpu.VMEM((16, b.shape[1]), BF16),
        pltpu.VMEM((16, c.shape[1]), BF16),
        pltpu.VMEM(x.shape, F32),
        pltpu.VMEM(x.shape, F32),
        pltpu.VMEM((STATE, channels), BF16),
        pltpu.VMEM((STATE, channels), BF16),
        pltpu.VMEM((STATE, half), BF16),
        pltpu.VMEM((STATE, half), BF16),
        pltpu.VMEM((STATE, half), BF16),
        pltpu.VMEM((STATE, half), BF16),
        pltpu.VMEM((STATE, half), BF16),
        pltpu.VMEM((8, 128), F32),
        pltpu.VMEM((8, 128), F32),
        pltpu.VMEM((8, 128), F32),
        pltpu.VMEM((8, 128), F32),
        pltpu.VMEM((8, TOK), F32),
        pltpu.VMEM((n_tp - 1, 8, TOK), F32),
        pltpu.VMEM((2 * TOK + 16, 128), BF16),
        pltpu.VMEM((3 * TOK, TOK), BF16),
        pltpu.VMEM((groups, TOK, TOK), BF16),
        pltpu.VMEM((groups, STATE, TOK), BF16),
        pltpu.VMEM((groups, TOK, STATE), BF16),
        pltpu.VMEM((TOK, 128), BF16),
        pltpu.VMEM((5, TOK, 128), BF16),
        pltpu.VMEM((TOK, TOK), F32),
        pltpu.VMEM(q.shape, BF16),
        pltpu.VMEM(x.shape, BF16),
        pltpu.VMEM((TOK, 128), F32),
        pltpu.SemaphoreType.DMA((COPIES,)),
        pltpu.SemaphoreType.DMA((COPIES,)),
        pltpu.SemaphoreType.DMA((9,)),
    ]
    return pl.pallas_call(
        functools.partial(kernel, n_ctx, n_tp),
        out_shape=(
            jax.ShapeDtypeStruct(q.shape, BF16),
            jax.ShapeDtypeStruct(x.shape, BF16),
        ),
        in_specs=specs,
        out_specs=(hbm, hbm),
        scratch_shapes=scratch,
        compiler_params=pltpu.CompilerParams(
            collective_id=1, has_side_effects=True, vmem_limit_bytes=56 * 2**20
        ),
        name="packed_mix",
    )(
        q,
        k,
        v,
        ids.reshape(-1, 128),
        x,
        b,
        c,
        z,
        dt_raw,
        conv_x,
        conv_b,
        conv_c,
        dt_bias[None],
        rates[None],
        skip_d[None],
        gain[None],
    )


def solution(mesh):
    both = P("ctx", "tp")
    placed = (both, both, both, P(), both, both, both, both, both)
    placed += (P(None, "tp"),) * 3 + (P("tp"),) * 4
    return jax.shard_map(
        per_device, mesh=mesh, in_specs=placed, out_specs=(both, both), check_vma=False
    )
```

profile of v0, /device:TPU:38, one launch (start us, length us, event | category | flops | bytes accessed | tf_op | source)
XLA Modules:
  0.0 75.4 jit_solution(8196883105043489753)
XLA Ops:
  0.6 1.5 %copy.18.dt_raw = bf16[256,64]{1,0:T(8,128)(2,1)} copy(bf16[256,64]{0,1:T(8,128)(2,1)} %param.24) | data formatting | bytes 65536 | tf_op args[8]
  2.1 69.5 %packed_mix.1 = (bf16[256,2048]{1,0:T(8,128)(2,1)}, bf16[256,4096]{1,0:T(8,128)(2,1)}) custom-call(bf16[256,2048]{1,0:T(8,128)(2,1)} %q_hbm.1, bf16[256,256]{1,0:T(8,128)(2,1)} %k_hbm.1, bf16[256,256]{1,0:T(8,128)(2,1)} %v_hbm.1, s32[64,128]{1,0:T(8,128)} %bitcast.5, bf16[256,4096]{1,0:T(8,128)(2,1)} %x_hbm.1, bf16[256,256]{1,0:T(8,128)(2,1)} %b_hbm.1, ...), custom_call_target="tpu_custom_call" | custom-call | tf_op jit(solution)/shard_map/packed_mix/pallas_call | solution.py:527
  71.6 0.0 copy-start
  71.6 2.5 %copy.21 = bf16[256,2048]{1,0:T(8,128)(2,1)} copy(bf16[256,2048]{1,0:T(8,128)(2,1)} %get-tuple-element.4) | data formatting | bytes 2097152
  74.1 0.0 copy-done
  74.1 1.3 %copy.22 = bf16[256,4096]{1,0:T(8,128)(2,1)} copy(bf16[256,4096]{1,0:T(8,128)(2,1)S(1)} %copy-done) | data formatting | bytes 4194304
Async XLA Ops:
  71.6 2.5 %copy-start = (bf16[256,4096]{1,0:T(8,128)(2,1)S(1)}, bf16[256,4096]{1,0:T(8,128)(2,1)}, u32[]{:S(2)}) copy-start(bf16[256,4096]{1,0:T(8,128)(2,1)} %get-tuple-element.5) | copy-start | bytes 6291460
where the time goes:
time: 75.6 us; the launch traced here: 75.4 us
  Pallas kernels  69.5 us (92%)
  local copies, waits for them, and re-layouts  5.27 us (7%)
    pallas_call x1, Pallas kernels, per_device(): pl.pallas_call(functools.partial(kernel, n_ctx, n_tp), out_shape=(jax.Sha...  69.5 us
    unnamed x5, local copies, waits for them, and re-layouts  5.27 us

commit v1 on v0

--- a/solution.py
+++ b/solution.py
@@ -16,11 +16,18 @@
 
 TOK = 256
 WIDE = 512
+Z_CHIPS = 4
 MESH = pl.DeviceIdType.MESH
 F32 = jnp.float32
 BF16 = jnp.bfloat16
 
-RIM_X, RIM_B, RIM_C, K1, V1, K2, V2, KX, VX, K1S, V1S, E_SIB, T_SIB, E_C1, E_C2, T_C, IN_SIB, SQ = range(18)
+CHUNKS = 4
+RIM_X, RIM_B, RIM_C, K1, V1, KZ, K2, V2, KX, VX, K1S, V1S, E_A, E_B, T_SIB, T_C = range(16)
+E1 = 16
+EZ = E1 + CHUNKS
+E2 = EZ + CHUNKS
+IN = E2 + CHUNKS
+SQ = IN + CHUNKS
 COPIES = SQ + 3
 L_X, L_Z, L_Q, L_K, L_V, L_B, L_C, L_AO, L_MO = range(9)
 
@@ -44,7 +51,8 @@
 
 def split2(a):
     high = a.astype(BF16).astype(F32)
-    return jnp.concatenate([high, a - high], axis=1).astype(BF16)
+    lane = lax.broadcasted_iota(jnp.int32, a.shape, 1)
+    return jnp.where(lane < 64, high, a - high).astype(BF16)
 
 
 def kernel(
@@ -73,11 +81,13 @@
     qv,
     kbuf,
     vbuf,
+    k_pass,
     bv,
     cv,
     rim_x,
     rim_b,
     rim_c,
+    xs,
     g1,
     gate,
     e_own,
@@ -85,6 +95,7 @@
     e_chip,
     e_n1,
     e_n2,
+    e_pass,
     in_own,
     in_sib,
     t_own,
@@ -94,6 +105,8 @@
     sq_own,
     sq_in,
     expand,
+    expand_in,
+    spread_in,
     shift,
     mix,
     bt,
@@ -113,8 +126,22 @@
     core = lax.rem(p, 2)
     sib = p + 1 - 2 * core
     channels = x_hbm.shape[1]
-    groups = channels // 2048
-    half_width = channels // 2
+    groups = bv.shape[1] // STATE
+    tiles = channels // WIDE
+    per_group = tiles // groups
+    chip = p // 2
+    x_at, z_at = chip // Z_CHIPS, lax.rem(chip, Z_CHIPS)
+    x_chips = n_ctx // (2 * Z_CHIPS)
+
+    def chip_device(x, z):
+        return (lax.rem(x, x_chips) * Z_CHIPS + lax.rem(z, Z_CHIPS)) * 2 + core
+
+    wraps = ((z_at == 1) | (z_at == 2)).astype(jnp.int32)
+    pass_to = chip_device(x_at + wraps, z_at + Z_CHIPS - 1)
+    lower = chip_device(x_at, z_at + Z_CHIPS - 1)
+    upper = chip_device(x_at, z_at + 1)
+    upper_wraps = ((z_at == 0) | (z_at == 1)).astype(jnp.int32)
+    pass_from = chip_device(x_at + x_chips - upper_wraps, z_at + 1)
 
     def at(offset):
         return lax.rem(p + offset + n_ctx, n_ctx)
@@ -140,7 +167,7 @@
     }
 
     barrier = pltpu.get_barrier_semaphore()
-    for source in (sib, at(-1), at(-2), at(-4)):
+    for source in (sib, at(-1), at(-2), upper, pass_from):
         pl.semaphore_signal(barrier, inc=1, device_id=(source, t), device_id_type=MESH)
     for step in range(1, n_tp):
         pl.semaphore_signal(
@@ -148,7 +175,7 @@
         )
     for slot in (L_B, L_C, L_X, L_Z, L_K, L_V, L_Q):
         loads[slot].start()
-    pl.semaphore_wait(barrier, 4 + n_tp - 1)
+    pl.semaphore_wait(barrier, 5 + n_tp - 1)
 
     last_rows = pl.ds(TOK - 16, 16)
     rims = [
@@ -159,15 +186,17 @@
     for copy in rims:
         copy.start()
     near = [
+        remote(v_hbm, vbuf.at[1], V1, at(2)),
         remote(k_hbm, kbuf.at[1], K1, at(2)),
-        remote(v_hbm, vbuf.at[1], V1, at(2)),
-    ]
+    ]
+    k_down = remote(k_hbm, k_pass, KZ, lower)
     far = [
-        remote(k_hbm, kbuf.at[3], K2, at(4)),
-        remote(v_hbm, vbuf.at[3], V2, at(4)),
-    ]
-    for copy in near + far:
+        remote(vbuf.at[1], vbuf.at[3], V2, at(2)),
+        remote(k_pass, kbuf.at[3], K2, pass_to),
+    ]
+    for copy in near:
         copy.start()
+    k_down.start()
     own_to_sib = [
         remote(k_hbm, kbuf.at[4], KX, sib),
         remote(v_hbm, vbuf.at[4], VX, sib),
@@ -218,9 +247,10 @@
         for back in range(1, 4)
     ]
 
-    raw = dt_raw[...].astype(F32) + dt_bias[...]
+    raw = dt_raw[...].astype(F32)
+    raw = jnp.concatenate([raw, raw], axis=0).T + repeat_lanes(dt_bias[...], 2)
     steps = jnp.maximum(raw, 0.0) + jnp.log(1.0 + jnp.exp(-jnp.abs(raw)))
-    log_decay = -steps * rates[...]
+    log_decay = -steps * repeat_lanes(rates[...], 2)
     upto = jnp.where(causal, 1.0, 0.0).astype(BF16)
     part = log_decay.astype(BF16)
     rest = log_decay - part.astype(F32)
@@ -233,12 +263,9 @@
     expand[pl.ds(TOK, TOK), :] = split2(jnp.exp(cum - middle))
     continues = before_id == last_id
     through = jnp.where(continues, jnp.exp(end), 0.0)
-    wide_through = jnp.concatenate([through, through], axis=1)
-    t_own[...] = jnp.broadcast_to(wide_through, (8, 128))
-    rows = lax.broadcasted_iota(jnp.int32, (16, 64), 0)
-    vectors = jnp.where(rows == 0, jnp.exp(end - middle), jnp.where(rows == 1, skip_d[...], 0.0))
-    expand[pl.ds(2 * TOK, 16), :] = split2(vectors)
-    middle_factor = jnp.exp(middle)
+    t_own[...] = jnp.broadcast_to(through, (8, 128))
+    t_send = remote(t_own, t_sib, T_SIB, sib)
+    t_send.start()
 
     def spread_matrix(tile):
         head = lax.broadcasted_iota(jnp.int32, (128, WIDE), 0) & 63
@@ -261,7 +288,7 @@
 
     for slot in (L_B, L_C):
         loads[slot].wait()
-    for copy in rims:
+    for copy in rims[:2]:
         copy.wait()
     b_conv = conv(bv[...], rim_b[...], conv_b[...], bv.shape[1])
     c_conv = conv(cv[...], rim_c[...], conv_c[...], cv.shape[1])
@@ -273,67 +300,84 @@
         bt[group] = ending.T.astype(BF16)
         cj[group] = jnp.where(own_cols == before_id, c_group.astype(F32), 0.0).astype(BF16)
 
+    t_send.wait()
+    t_chip[...] = t_own[...] * t_sib[...]
+    t_next = remote(t_chip, t_n1, T_C, at(2))
+    t_next.start()
+    is_low = core == 0
+    rows = lax.broadcasted_iota(jnp.int32, (16, 128), 0)
+    vectors = jnp.where(rows == 0, jnp.exp(end - middle), 0.0)
+    vectors = jnp.where(rows == 1, repeat_lanes(skip_d[...], 2), vectors)
+    vectors = jnp.where(rows == 2, jnp.where(is_low, t_sib[0:1], 1.0), vectors)
+    vectors = jnp.where(rows == 3, jnp.where(is_low, 1.0, t_own[0:1]), vectors)
+    expand[pl.ds(2 * TOK, 16), :] = split2(vectors)
+
     loads[L_X].wait()
-    loads[L_Z].wait()
-    tiles_per_group = 2048 // WIDE
-
-    def ssd_tile(tile, carry):
-        group = tile // tiles_per_group
+    rims[2].wait()
+
+    def end_state(tile):
         here = pl.ds(pl.multiple_of(tile * WIDE, WIDE), WIDE)
         x_conv = conv(xv[:, here], rim_x[:, here], conv_x[:, here], WIDE)
-        factors = dot(expand[...], spread_matrix(tile))
-        x_wide = x_conv.astype(F32)
-        x_scaled = (x_wide * factors[:TOK]).astype(BF16)
-        inside = dot(mix[group], x_scaled)
-        e_own[:, here] = (dot(bt[group], x_scaled) * factors[2 * TOK : 2 * TOK + 1]).astype(BF16)
-        open_gate = silu(zv[:, here].astype(F32))
-        leaving = factors[TOK : 2 * TOK]
-        full = leaving * inside + factors[2 * TOK + 1 : 2 * TOK + 2] * x_wide
-        g1[:, here] = full * open_gate
-        gate[:, here] = leaving * open_gate
+        xv[:, here] = x_conv
+        spread = spread_matrix(tile)
+        factors = dot(expand[pl.ds(0, TOK), :], spread)
+        vectors = dot(expand[pl.ds(2 * TOK, 16), :], spread)
+        x_scaled = (x_conv.astype(F32) * factors).astype(BF16)
+        xs[:, here] = x_scaled
+        state = dot(bt[tile // per_group], x_scaled) * vectors[0:1]
+        e_own[tile] = state.astype(BF16)
+        return state, vectors
+
+    mine, others = core * CHUNKS, (1 - core) * CHUNKS
+
+    def other_half(chunk, carry):
+        end_state(others + chunk)
         return carry
 
-    lax.fori_loop(0, channels // WIDE, ssd_tile, 0)
-
-    to_sib = [remote(e_own, e_sib, E_SIB, sib), remote(t_own, t_sib, T_SIB, sib)]
-    for copy in to_sib:
-        copy.start()
-    for copy in near:
+    lax.fori_loop(0, CHUNKS, other_half, 0, unroll=2)
+    half_a = remote(e_own.at[pl.ds(others, CHUNKS)], e_sib.at[pl.ds(others, CHUNKS)], E_A, sib)
+    half_a.start()
+
+    for copy in near + [k_down]:
         copy.wait()
     sib_near = [
         remote(kbuf.at[1], kbuf.at[2], K1S, sib),
         remote(vbuf.at[1], vbuf.at[2], V1S, sib),
     ]
-    for copy in sib_near:
+    for copy in far + sib_near:
         copy.start()
-    for copy in to_sib:
-        copy.wait()
-
-    t_chip[...] = t_own[...] * t_sib[...]
-    is_low = core == 0
-    u_own = split2(jnp.where(is_low, t_sib[...], 1.0)[:, :64])
-    u_sib = split2(jnp.where(is_low, 1.0, t_own[...])[:, :64])
-    u_both = jnp.concatenate([u_own, u_sib], axis=0)
-    half_tiles = half_width // WIDE
-
-    def chip_tile(tile, carry):
-        whole = core * half_tiles + tile
+
+    nears = [remote(e_chip.at[i], e_n1.at[i], E1 + i, at(2)) for i in range(CHUNKS)]
+    downs = [remote(e_chip.at[i], e_pass.at[i], EZ + i, lower) for i in range(1, CHUNKS)]
+    for chunk in range(CHUNKS):
+        state, vectors = end_state(mine + chunk)
+        if chunk == 0:
+            half_a.wait()
+        e_chip[chunk] = (
+            vectors[2:3] * state + vectors[3:4] * e_sib[mine + chunk].astype(F32)
+        ).astype(BF16)
+        nears[chunk].start()
+        if chunk:
+            downs[chunk - 1].start()
+    half_b = remote(e_own.at[pl.ds(mine, CHUNKS)], e_sib.at[pl.ds(mine, CHUNKS)], E_B, sib)
+    half_b.start()
+
+    loads[L_Z].wait()
+
+    def gate_tile(tile, carry):
         here = pl.ds(pl.multiple_of(tile * WIDE, WIDE), WIDE)
-        there = pl.ds(pl.multiple_of(whole * WIDE, WIDE), WIDE)
-        factors = dot(u_both, spread_matrix(whole))
-        e_chip[:, here] = (
-            factors[0:1] * e_own[:, there].astype(F32) + factors[8:9] * e_sib[:, there].astype(F32)
-        ).astype(BF16)
+        spread = spread_matrix(tile)
+        leaving = dot(expand[pl.ds(TOK, TOK), :], spread)
+        vectors = dot(expand[pl.ds(2 * TOK, 16), :], spread)
+        open_gate = silu(zv[:, here].astype(F32))
+        full = leaving * dot(mix[tile // per_group], xs[:, here]) + vectors[1:2] * xv[
+            :, here
+        ].astype(F32)
+        g1[:, here] = full * open_gate
+        gate[:, here] = leaving * open_gate
         return carry
 
-    lax.fori_loop(0, half_tiles, chip_tile, 0)
-    chip_sends = [
-        remote(t_chip, t_n1, T_C, at(2)),
-        remote(e_chip, e_n1, E_C1, at(2)),
-        remote(e_chip, e_n2, E_C2, at(4)),
-    ]
-    for copy in chip_sends:
-        copy.start()
+    lax.fori_loop(0, tiles, gate_tile, 0, unroll=2)
 
     for copy in far:
         copy.wait()
@@ -346,6 +390,7 @@
     def _():
         for copy in far_to_sib:
             copy.start()
+        for copy in far_to_sib:
             copy.wait_send()
 
     @pl.when(core == 0)
@@ -384,55 +429,71 @@
         ao[:, here] = (summed[:, :HEAD_DIM] / summed[:, HEAD_DIM:]).astype(BF16)
         return carry
 
-    lax.fori_loop(0, query_heads, attend, 0)
+    per_part = query_heads // CHUNKS
+
+    def attend_part(part, carry):
+        lax.fori_loop(part * per_part, (part + 1) * per_part, attend, 0, unroll=True)
+
+        @pl.when(part < CHUNKS - 1)
+        def _():
+            remote(e_chip.at[part], e_pass.at[part + 1], EZ + part + 1, lower).wait_recv()
+            remote(e_pass.at[part + 1], e_n2.at[part + 1], E2 + part + 1, pass_to).start()
+
+        @pl.when(part == 0)
+        def _():
+            nears[0].wait_recv()
+            remote(e_n1.at[0], e_n2.at[0], E2, at(2)).start()
+
+        return carry
+
+    lax.fori_loop(0, CHUNKS, attend_part, 0)
     ao_out = pltpu.make_async_copy(ao, ao_hbm, local.at[L_AO])
     ao_out.start()
 
-    for copy in chip_sends:
-        copy.wait()
-    u_chip = split2(t_n1[...][:, :64])
-
-    def in_tile(tile, carry):
+    t_next.wait()
+    half_b.wait()
+    vectors = jnp.where(rows == 0, jnp.where(is_low, 0.0, jnp.exp(middle)), 0.0)
+    vectors = jnp.where(rows == 1, jnp.where(is_low, 1.0, t_sib[0:1]) * jnp.exp(middle), vectors)
+    vectors = jnp.where(rows == 2, t_n1[0:1], vectors)
+    expand_in[...] = split2(vectors)
+
+    def spread_tile(tile, carry):
+        spread_in[tile] = dot(expand_in[...], spread_matrix(tile))
+        return carry
+
+    lax.fori_loop(0, tiles, spread_tile, 0)
+    sumsq[...] = jnp.zeros_like(sumsq)
+
+    def join_tile(tile, incoming):
         here = pl.ds(pl.multiple_of(tile * WIDE, WIDE), WIDE)
-        factors = dot(u_chip, spread_matrix(core * half_tiles + tile))
-        in_own[:, here] = (
-            e_n1[:, here].astype(F32) + factors[0:1] * e_n2[:, here].astype(F32)
-        ).astype(BF16)
-        return carry
-
-    lax.fori_loop(0, half_tiles, in_tile, 0)
-    swap = remote(in_own, in_sib, IN_SIB, sib)
-    swap.start()
-
-    w_sib = split2(jnp.where(is_low, 0.0, jnp.broadcast_to(middle_factor, (8, 64))))
-    w_in = split2(jnp.where(is_low, 1.0, t_sib[...])[:, :64] * middle_factor)
-    w_both = jnp.concatenate([w_sib, w_in], axis=0)
-    sumsq[...] = jnp.zeros_like(sumsq)
-
-    def join_tiles(incoming, first):
-        def join_tile(tile, carry):
-            whole = first + tile
-            group = whole // tiles_per_group
-            here = pl.ds(pl.multiple_of(tile * WIDE, WIDE), WIDE)
-            there = pl.ds(pl.multiple_of(whole * WIDE, WIDE), WIDE)
-            factors = dot(w_both, spread_matrix(whole))
-            state = factors[0:1] * e_sib[:, there].astype(F32) + factors[8:9] * incoming[
-                :, here
-            ].astype(F32)
-            gated = g1[:, there] + gate[:, there] * dot(cj[group], state.astype(BF16))
-            g1[:, there] = gated
-            squares = gated * gated
-            total = sumsq[...]
-            for lane in range(WIDE // 128):
-                total = total + squares[:, lane * 128 : (lane + 1) * 128]
-            sumsq[...] = total
-            return carry
-
-        lax.fori_loop(0, half_tiles, join_tile, 0)
-
-    join_tiles(in_own, core * half_tiles)
-    swap.wait()
-    join_tiles(in_sib, (1 - core) * half_tiles)
+        vectors = spread_in[tile]
+        state = vectors[0:1] * e_sib[tile].astype(F32) + vectors[1:2] * incoming
+        gated = g1[:, here] + gate[:, here] * dot(cj[tile // per_group], state.astype(BF16))
+        g1[:, here] = gated
+        squares = gated * gated
+        total = sumsq[...]
+        for lane in range(WIDE // 128):
+            total = total + squares[:, lane * 128 : (lane + 1) * 128]
+        sumsq[...] = total
+
+    swaps = [remote(in_own.at[i], in_sib.at[i], IN + i, sib) for i in range(CHUNKS)]
+    for chunk in range(CHUNKS):
+        tile = mine + chunk
+        if chunk == 0:
+            passed = remote(e_n1.at[0], e_n2.at[0], E2, at(2))
+            nears[0].wait_send()
+        else:
+            passed = remote(e_pass.at[chunk], e_n2.at[chunk], E2 + chunk, pass_to)
+            nears[chunk].wait()
+            downs[chunk - 1].wait_send()
+        passed.wait()
+        arriving = e_n1[chunk].astype(F32) + spread_in[tile][2:3] * e_n2[chunk].astype(F32)
+        in_own[chunk] = arriving.astype(BF16)
+        swaps[chunk].start()
+        join_tile(tile, arriving)
+    for chunk in range(CHUNKS):
+        swaps[chunk].wait()
+        join_tile(others + chunk, in_sib[chunk].astype(F32))
 
     own_sums = jnp.concatenate(
         [
@@ -463,22 +524,26 @@
     )
     scale_wide = repeat_lanes(scale_cols, WIDE // 128)
 
-    def norm_tile(tile, carry):
-        here = pl.ds(pl.multiple_of(tile * WIDE, WIDE), WIDE)
+    outs = []
+    for tile in range(tiles):
+        here = slice(tile * WIDE, (tile + 1) * WIDE)
         mo[:, here] = (g1[:, here] * scale_wide * gain[:, here]).astype(BF16)
-        return carry
-
-    lax.fori_loop(0, channels // WIDE, norm_tile, 0)
-    mo_out = pltpu.make_async_copy(mo, mo_hbm, local.at[L_MO])
-    mo_out.start()
+        out = pltpu.make_async_copy(
+            mo.at[:, pl.ds(tile * WIDE, WIDE)],
+            mo_hbm.at[:, pl.ds(tile * WIDE, WIDE)],
+            local.at[L_MO + tile],
+        )
+        out.start()
+        outs.append(out)
     ao_out.wait()
-    mo_out.wait()
+    for out in outs:
+        out.wait()
 
 
 def per_device(q, k, v, ids, x, b, c, z, dt_raw, conv_x, conv_b, conv_c, dt_bias, rates, skip_d, gain):
     n_ctx, n_tp = lax.axis_size("ctx"), lax.axis_size("tp")
     channels = x.shape[1]
-    half = channels // 2
+    tiles = channels // WIDE
     groups = b.shape[1] // STATE
     hbm = pl.BlockSpec(memory_space=pl.ANY)
     vmem = pl.BlockSpec(memory_space=pltpu.VMEM)
@@ -489,20 +554,23 @@
         pltpu.VMEM(q.shape, BF16),
         pltpu.VMEM((5,) + k.shape, BF16),
         pltpu.VMEM((5,) + v.shape, BF16),
+        pltpu.VMEM(k.shape, BF16),
         pltpu.VMEM(b.shape, BF16),
         pltpu.VMEM(c.shape, BF16),
         pltpu.VMEM((16, channels), BF16),
         pltpu.VMEM((16, b.shape[1]), BF16),
         pltpu.VMEM((16, c.shape[1]), BF16),
+        pltpu.VMEM(x.shape, BF16),
         pltpu.VMEM(x.shape, F32),
         pltpu.VMEM(x.shape, F32),
-        pltpu.VMEM((STATE, channels), BF16),
-        pltpu.VMEM((STATE, channels), BF16),
-        pltpu.VMEM((STATE, half), BF16),
-        pltpu.VMEM((STATE, half), BF16),
-        pltpu.VMEM((STATE, half), BF16),
-        pltpu.VMEM((STATE, half), BF16),
-        pltpu.VMEM((STATE, half), BF16),
+        pltpu.VMEM((tiles, STATE, WIDE), BF16),
+        pltpu.VMEM((tiles, STATE, WIDE), BF16),
+        pltpu.VMEM((CHUNKS, STATE, WIDE), BF16),
+        pltpu.VMEM((CHUNKS, STATE, WIDE), BF16),
+        pltpu.VMEM((CHUNKS, STATE, WIDE), BF16),
+        pltpu.VMEM((CHUNKS, STATE, WIDE), BF16),
+        pltpu.VMEM((CHUNKS, STATE, WIDE), BF16),
+        pltpu.VMEM((CHUNKS, STATE, WIDE), BF16),
         pltpu.VMEM((8, 128), F32),
         pltpu.VMEM((8, 128), F32),
         pltpu.VMEM((8, 128), F32),
@@ -510,6 +578,8 @@
         pltpu.VMEM((8, TOK), F32),
         pltpu.VMEM((n_tp - 1, 8, TOK), F32),
         pltpu.VMEM((2 * TOK + 16, 128), BF16),
+        pltpu.VMEM((16, 128), BF16),
+        pltpu.VMEM((tiles, 16, WIDE), F32),
         pltpu.VMEM((3 * TOK, TOK), BF16),
         pltpu.VMEM((groups, TOK, TOK), BF16),
         pltpu.VMEM((groups, STATE, TOK), BF16),
@@ -522,7 +592,7 @@
         pltpu.VMEM((TOK, 128), F32),
         pltpu.SemaphoreType.DMA((COPIES,)),
         pltpu.SemaphoreType.DMA((COPIES,)),
-        pltpu.SemaphoreType.DMA((9,)),
+        pltpu.SemaphoreType.DMA((L_MO + tiles,)),
     ]
     return pl.pallas_call(
         functools.partial(kernel, n_ctx, n_tp),
@@ -546,7 +616,7 @@
         b,
         c,
         z,
-        dt_raw,
+        dt_raw.T,
         conv_x,
         conv_b,
         conv_c,

time: 75.6 us -> 55.3 us (0.73)
  the two profiles are of different devices: /device:TPU:38 before, /device:TPU:1 now
where the time goes in v1:
time: 55.3 us; the launch traced here: 55.1 us
  Pallas kernels  50.7 us (92%)
  local copies, waits for them, and re-layouts  3.78 us (7%)
  between operations  0.65 us (1%)
    pallas_call x1, Pallas kernels, per_device(): pl.pallas_call(functools.partial(kernel, n_ctx, n_tp), out_shape=(jax.Sha...  50.7 us
    unnamed x4, local copies, waits for them, and re-layouts  3.78 us

profile of v1, /device:TPU:1, one launch (start us, length us, event | category | flops | bytes accessed | tf_op | source)
XLA Modules:
  0.0 55.1 jit_solution(8134505539128738761)
XLA Ops:
  0.6 50.7 %packed_mix.1 = (bf16[256,2048]{1,0:T(8,128)(2,1)}, bf16[256,4096]{1,0:T(8,128)(2,1)}) custom-call(bf16[256,2048]{1,0:T(8,128)(2,1)} %q_hbm.1, bf16[256,256]{1,0:T(8,128)(2,1)} %k_hbm.1, bf16[256,256]{1,0:T(8,128)(2,1)} %v_hbm.1, s32[64,128]{1,0:T(8,128)} %bitcast.6, bf16[256,4096]{1,0:T(8,128)(2,1)} %x_hbm.1, bf16[256,256]{1,0:T(8,128)(2,1)} %b_hbm.1, ...), custom_call_target="tpu_custom_call" | custom-call | tf_op jit(solution)/shard_map/packed_mix/pallas_call | solution.py:597
  51.3 0.0 copy-start
  51.4 2.5 %copy.20 = bf16[256,2048]{1,0:T(8,128)(2,1)} copy(bf16[256,2048]{1,0:T(8,128)(2,1)} %get-tuple-element.4) | data formatting | bytes 2097152
  53.8 0.0 copy-done
  53.8 1.3 %copy.21 = bf16[256,4096]{1,0:T(8,128)(2,1)} copy(bf16[256,4096]{1,0:T(8,128)(2,1)S(1)} %copy-done) | data formatting | bytes 4194304
Async XLA Ops:
  51.3 2.5 %copy-start = (bf16[256,4096]{1,0:T(8,128)(2,1)S(1)}, bf16[256,4096]{1,0:T(8,128)(2,1)}, u32[]{:S(2)}) copy-start(bf16[256,4096]{1,0:T(8,128)(2,1)} %get-tuple-element.5) | copy-start | bytes 6291460

commit v2 on v1

--- a/solution.py
+++ b/solution.py
@@ -22,11 +22,15 @@
 BF16 = jnp.bfloat16
 
 CHUNKS = 4
-RIM_X, RIM_B, RIM_C, K1, V1, KZ, K2, V2, KX, VX, K1S, V1S, E_A, E_B, T_SIB, T_C = range(16)
-E1 = 16
-EZ = E1 + CHUNKS
-E2 = EZ + CHUNKS
-IN = E2 + CHUNKS
+PIECE = 256
+PIECES = CHUNKS * WIDE // PIECE
+FORWARD = (0, 2, 4)
+RIM_X, RIM_B, RIM_C, K1, V1, KZ, K2, V2, KX, VX, K1S, V1S, E_B, T_SIB, T_C = range(15)
+E_A = 15
+E1 = E_A + CHUNKS
+EZ = E1 + PIECES
+E2 = EZ + PIECES
+IN = E2 + PIECES
 SQ = IN + CHUNKS
 COPIES = SQ + 3
 L_X, L_Z, L_Q, L_K, L_V, L_B, L_C, L_AO, L_MO = range(9)
@@ -224,17 +228,11 @@
     before_cols = jnp.where(first_device, -1.0, id_column(before_row))
     before_id = jnp.where(first_device, -1.0, id_row(before_row))[:, 127:128]
     lanes = lax.broadcasted_iota(jnp.int32, (TOK, 128), 1).astype(F32)
-    far_own[...] = jnp.where(own_cols == lanes, 0.0, -FAR).astype(BF16)
-    block_devices = (p, p - 2, p - 1 - 2 * core, p - 4, p - 3 + 2 * core)
-    for slot, device in enumerate(block_devices):
-        columns = id_columns(lax.rem(device + n_ctx, n_ctx)) if slot else own_cols
-        hot[slot] = jnp.where(columns == lanes, 1.0, 0.0).astype(BF16)
     row_at = lax.broadcasted_iota(jnp.int32, (TOK, TOK), 0)
     col_at = lax.broadcasted_iota(jnp.int32, (TOK, TOK), 1)
     same = repeat_lanes(own_cols, 2) == own_row
     causal = col_at <= row_at
     allowed = same & causal
-    tri_bias[...] = jnp.where(causal, 0.0, -FAR)
     for back in range(1, 4):
         shift[pl.ds((back - 1) * TOK, TOK), :] = jnp.where(
             same & (row_at - col_at == back), 1.0, 0.0
@@ -286,19 +284,13 @@
         total = jnp.concatenate([total[:8] + edge, total[8:]], axis=0)
         return silu(total).astype(BF16)
 
-    for slot in (L_B, L_C):
-        loads[slot].wait()
-    for copy in rims[:2]:
-        copy.wait()
+    loads[L_B].wait()
+    rims[0].wait()
     b_conv = conv(bv[...], rim_b[...], conv_b[...], bv.shape[1])
-    c_conv = conv(cv[...], rim_c[...], conv_c[...], cv.shape[1])
     for group in range(groups):
         b_group = b_conv[:, group * STATE : (group + 1) * STATE]
-        c_group = c_conv[:, group * STATE : (group + 1) * STATE]
-        mix[group] = jnp.where(allowed, dot_nt(c_group, b_group), 0.0).astype(BF16)
         ending = jnp.where(own_cols == last_id, b_group.astype(F32), 0.0)
         bt[group] = ending.T.astype(BF16)
-        cj[group] = jnp.where(own_cols == before_id, c_group.astype(F32), 0.0).astype(BF16)
 
     t_send.wait()
     t_chip[...] = t_own[...] * t_sib[...]
@@ -330,37 +322,74 @@
 
     mine, others = core * CHUNKS, (1 - core) * CHUNKS
 
-    def other_half(chunk, carry):
-        end_state(others + chunk)
-        return carry
-
-    lax.fori_loop(0, CHUNKS, other_half, 0, unroll=2)
-    half_a = remote(e_own.at[pl.ds(others, CHUNKS)], e_sib.at[pl.ds(others, CHUNKS)], E_A, sib)
-    half_a.start()
-
-    for copy in near + [k_down]:
-        copy.wait()
+    k_down.wait()
+    far[1].start()
+    halves = [
+        remote(e_own.at[others + i], e_sib.at[others + i], E_A + i, sib) for i in range(CHUNKS)
+    ]
+    nears = [remote(e_chip.at[i], e_n1.at[i], E1 + i, at(2)) for i in range(PIECES)]
+    downs = [
+        None if i in FORWARD else remote(e_chip.at[i], e_pass.at[i], EZ + i, lower)
+        for i in range(PIECES)
+    ]
+    passes = [
+        remote(e_n1.at[i], e_n2.at[i], E2 + i, at(2))
+        if i in FORWARD
+        else remote(e_pass.at[i], e_n2.at[i], E2 + i, pass_to)
+        for i in range(PIECES)
+    ]
+
+    def pass_on(*pieces):
+        for i in pieces:
+            (nears[i] if i in FORWARD else downs[i]).wait_recv()
+            passes[i].start()
+
+    for step in range(CHUNKS + 1):
+        if step < CHUNKS:
+            end_state(others + step)
+            halves[step].start()
+        if step == 1:
+            near[0].wait()
+            far[0].start()
+        if step == 0:
+            continue
+        chunk = step - 1
+        state, vectors = end_state(mine + chunk)
+        halves[chunk].wait()
+        chip_end = (
+            vectors[2:3] * state + vectors[3:4] * e_sib[mine + chunk].astype(F32)
+        ).astype(BF16)
+        for i in range(WIDE // PIECE):
+            piece = chunk * (WIDE // PIECE) + i
+            e_chip[piece] = chip_end[:, i * PIECE : (i + 1) * PIECE]
+            nears[piece].start()
+            if downs[piece] is not None:
+                downs[piece].start()
+    half_b = remote(e_own.at[pl.ds(mine, CHUNKS)], e_sib.at[pl.ds(mine, CHUNKS)], E_B, sib)
+    half_b.start()
+    near[1].wait()
     sib_near = [
         remote(kbuf.at[1], kbuf.at[2], K1S, sib),
         remote(vbuf.at[1], vbuf.at[2], V1S, sib),
     ]
-    for copy in far + sib_near:
+    for copy in sib_near:
         copy.start()
 
-    nears = [remote(e_chip.at[i], e_n1.at[i], E1 + i, at(2)) for i in range(CHUNKS)]
-    downs = [remote(e_chip.at[i], e_pass.at[i], EZ + i, lower) for i in range(1, CHUNKS)]
-    for chunk in range(CHUNKS):
-        state, vectors = end_state(mine + chunk)
-        if chunk == 0:
-            half_a.wait()
-        e_chip[chunk] = (
-            vectors[2:3] * state + vectors[3:4] * e_sib[mine + chunk].astype(F32)
-        ).astype(BF16)
-        nears[chunk].start()
-        if chunk:
-            downs[chunk - 1].start()
-    half_b = remote(e_own.at[pl.ds(mine, CHUNKS)], e_sib.at[pl.ds(mine, CHUNKS)], E_B, sib)
-    half_b.start()
+    loads[L_C].wait()
+    rims[1].wait()
+    c_conv = conv(cv[...], rim_c[...], conv_c[...], cv.shape[1])
+    for group in range(groups):
+        b_group = b_conv[:, group * STATE : (group + 1) * STATE]
+        c_group = c_conv[:, group * STATE : (group + 1) * STATE]
+        mix[group] = jnp.where(allowed, dot_nt(c_group, b_group), 0.0).astype(BF16)
+        cj[group] = jnp.where(own_cols == before_id, c_group.astype(F32), 0.0).astype(BF16)
+
+    far_own[...] = jnp.where(own_cols == lanes, 0.0, -FAR).astype(BF16)
+    block_devices = (p, p - 2, p - 1 - 2 * core, p - 4, p - 3 + 2 * core)
+    for slot, device in enumerate(block_devices):
+        columns = id_columns(lax.rem(device + n_ctx, n_ctx)) if slot else own_cols
+        hot[slot] = jnp.where(columns == lanes, 1.0, 0.0).astype(BF16)
+    tri_bias[...] = jnp.where(causal, 0.0, -FAR)
 
     loads[L_Z].wait()
 
@@ -377,7 +406,10 @@
         gate[:, here] = leaving * open_gate
         return carry
 
-    lax.fori_loop(0, tiles, gate_tile, 0, unroll=2)
+    lax.fori_loop(0, tiles // 2, gate_tile, 0, unroll=2)
+    pass_on(0, 1)
+    lax.fori_loop(tiles // 2, tiles, gate_tile, 0, unroll=2)
+    pass_on(2, 3)
 
     for copy in far:
         copy.wait()
@@ -431,25 +463,6 @@
 
     per_part = query_heads // CHUNKS
 
-    def attend_part(part, carry):
-        lax.fori_loop(part * per_part, (part + 1) * per_part, attend, 0, unroll=True)
-
-        @pl.when(part < CHUNKS - 1)
-        def _():
-            remote(e_chip.at[part], e_pass.at[part + 1], EZ + part + 1, lower).wait_recv()
-            remote(e_pass.at[part + 1], e_n2.at[part + 1], E2 + part + 1, pass_to).start()
-
-        @pl.when(part == 0)
-        def _():
-            nears[0].wait_recv()
-            remote(e_n1.at[0], e_n2.at[0], E2, at(2)).start()
-
-        return carry
-
-    lax.fori_loop(0, CHUNKS, attend_part, 0)
-    ao_out = pltpu.make_async_copy(ao, ao_hbm, local.at[L_AO])
-    ao_out.start()
-
     t_next.wait()
     half_b.wait()
     vectors = jnp.where(rows == 0, jnp.where(is_low, 0.0, jnp.exp(middle)), 0.0)
@@ -477,40 +490,68 @@
         sumsq[...] = total
 
     swaps = [remote(in_own.at[i], in_sib.at[i], IN + i, sib) for i in range(CHUNKS)]
-    for chunk in range(CHUNKS):
-        tile = mine + chunk
-        if chunk == 0:
-            passed = remote(e_n1.at[0], e_n2.at[0], E2, at(2))
-            nears[0].wait_send()
-        else:
-            passed = remote(e_pass.at[chunk], e_n2.at[chunk], E2 + chunk, pass_to)
-            nears[chunk].wait()
-            downs[chunk - 1].wait_send()
-        passed.wait()
-        arriving = e_n1[chunk].astype(F32) + spread_in[tile][2:3] * e_n2[chunk].astype(F32)
-        in_own[chunk] = arriving.astype(BF16)
-        swaps[chunk].start()
-        join_tile(tile, arriving)
-    for chunk in range(CHUNKS):
-        swaps[chunk].wait()
-        join_tile(others + chunk, in_sib[chunk].astype(F32))
-
-    own_sums = jnp.concatenate(
-        [
-            jnp.sum(sumsq[pl.ds(0, 128), :].T, axis=0, keepdims=True),
-            jnp.sum(sumsq[pl.ds(128, 128), :].T, axis=0, keepdims=True),
-        ],
-        axis=1,
-    )
-    sq_own[...] = jnp.broadcast_to(own_sums, (8, TOK))
     sq_sends = [
         remote(sq_own, sq_in.at[step - 1], SQ + step - 1, p, lax.rem(t + step, n_tp))
         for step in range(1, n_tp)
     ]
-    for copy in sq_sends:
-        copy.start()
+
+    def join_all():
+        for chunk in range(CHUNKS):
+            tile = mine + chunk
+            pieces = range(chunk * (WIDE // PIECE), (chunk + 1) * (WIDE // PIECE))
+            for i in pieces:
+                if i not in FORWARD:
+                    nears[i].wait_recv()
+                passes[i].wait_recv()
+            near_end = jnp.concatenate([e_n1[i] for i in pieces], axis=1).astype(F32)
+            far_end = jnp.concatenate([e_n2[i] for i in pieces], axis=1).astype(F32)
+            arriving = near_end + spread_in[tile][2:3] * far_end
+            in_own[chunk] = arriving.astype(BF16)
+            swaps[chunk].start()
+            join_tile(tile, arriving)
+        for chunk in range(CHUNKS):
+            swaps[chunk].wait()
+            join_tile(others + chunk, in_sib[chunk].astype(F32))
+
+        own_sums = jnp.concatenate(
+            [
+                jnp.sum(sumsq[pl.ds(0, 128), :].T, axis=0, keepdims=True),
+                jnp.sum(sumsq[pl.ds(128, 128), :].T, axis=0, keepdims=True),
+            ],
+            axis=1,
+        )
+        sq_own[...] = jnp.broadcast_to(own_sums, (8, TOK))
+        for copy in sq_sends:
+            copy.start()
+
+    def attend_part(part, carry):
+        for i in range(per_part):
+            attend(part * per_part + i, carry)
+
+        @pl.when(part == 0)
+        def _():
+            pass_on(4, 5)
+
+        @pl.when(part == 1)
+        def _():
+            pass_on(6, 7)
+
+        @pl.when(part == CHUNKS - 2)
+        def _():
+            join_all()
+
+        return carry
+
+    lax.fori_loop(0, CHUNKS, attend_part, 0)
+    ao_out = pltpu.make_async_copy(ao, ao_hbm, local.at[L_AO])
+    ao_out.start()
     for copy in sq_sends:
         copy.wait()
+    for i in range(PIECES):
+        nears[i].wait_send()
+        passes[i].wait_send()
+        if downs[i] is not None:
+            downs[i].wait_send()
     total = sq_own[...]
     for step in range(1, n_tp):
         total = total + sq_in[step - 1]
@@ -565,10 +606,10 @@
         pltpu.VMEM(x.shape, F32),
         pltpu.VMEM((tiles, STATE, WIDE), BF16),
         pltpu.VMEM((tiles, STATE, WIDE), BF16),
-        pltpu.VMEM((CHUNKS, STATE, WIDE), BF16),
-        pltpu.VMEM((CHUNKS, STATE, WIDE), BF16),
-        pltpu.VMEM((CHUNKS, STATE, WIDE), BF16),
-        pltpu.VMEM((CHUNKS, STATE, WIDE), BF16),
+        pltpu.VMEM((PIECES, STATE, PIECE), BF16),
+        pltpu.VMEM((PIECES, STATE, PIECE), BF16),
+        pltpu.VMEM((PIECES, STATE, PIECE), BF16),
+        pltpu.VMEM((PIECES, STATE, PIECE), BF16),
         pltpu.VMEM((CHUNKS, STATE, WIDE), BF16),
         pltpu.VMEM((CHUNKS, STATE, WIDE), BF16),
         pltpu.VMEM((8, 128), F32),

time: 55.3 us -> 49.5 us (0.90)
  Pallas kernels: 50.7 us -> 44.9 us
    pallas_call x1, Pallas kernels: 50.7 us -> 44.9 us  [per_device(): pl.pallas_call(functools.partial(kernel, n_ctx, n_tp), out_shape=(jax.Sha...]
where the time goes in v2:
time: 49.5 us; the launch traced here: 49.3 us
  Pallas kernels  44.9 us (91%)
  local copies, waits for them, and re-layouts  3.78 us (8%)
  between operations  0.65 us (1%)
    pallas_call x1, Pallas kernels, per_device(): pl.pallas_call(functools.partial(kernel, n_ctx, n_tp), out_shape=(jax.Sha...  44.9 us
    unnamed x4, local copies, waits for them, and re-layouts  3.78 us

profile of v2, /device:TPU:1, one launch (start us, length us, event | category | flops | bytes accessed | tf_op | source)
XLA Modules:
  0.0 49.3 jit_solution(10479982955453699421)
XLA Ops:
  0.6 44.9 %packed_mix.1 = (bf16[256,2048]{1,0:T(8,128)(2,1)}, bf16[256,4096]{1,0:T(8,128)(2,1)}) custom-call(bf16[256,2048]{1,0:T(8,128)(2,1)} %q_hbm.1, bf16[256,256]{1,0:T(8,128)(2,1)} %k_hbm.1, bf16[256,256]{1,0:T(8,128)(2,1)} %v_hbm.1, s32[64,128]{1,0:T(8,128)} %bitcast.6, bf16[256,4096]{1,0:T(8,128)(2,1)} %x_hbm.1, bf16[256,256]{1,0:T(8,128)(2,1)} %b_hbm.1, ...), custom_call_target="tpu_custom_call" | custom-call | tf_op jit(solution)/shard_map/packed_mix/pallas_call | solution.py:638
  45.5 0.0 copy-start
  45.5 2.5 %copy.20 = bf16[256,2048]{1,0:T(8,128)(2,1)} copy(bf16[256,2048]{1,0:T(8,128)(2,1)} %get-tuple-element.4) | data formatting | bytes 2097152
  48.0 0.0 copy-done
  48.0 1.3 %copy.21 = bf16[256,4096]{1,0:T(8,128)(2,1)} copy(bf16[256,4096]{1,0:T(8,128)(2,1)S(1)} %copy-done) | data formatting | bytes 4194304
Async XLA Ops:
  45.5 2.5 %copy-start = (bf16[256,4096]{1,0:T(8,128)(2,1)S(1)}, bf16[256,4096]{1,0:T(8,128)(2,1)}, u32[]{:S(2)}) copy-start(bf16[256,4096]{1,0:T(8,128)(2,1)} %get-tuple-element.5) | copy-start | bytes 6291460

commit v3 on v2

--- a/solution.py
+++ b/solution.py
@@ -16,6 +16,7 @@
 
 TOK = 256
 WIDE = 512
+PARTS = 4
 Z_CHIPS = 4
 MESH = pl.DeviceIdType.MESH
 F32 = jnp.float32
@@ -24,7 +25,6 @@
 CHUNKS = 4
 PIECE = 256
 PIECES = CHUNKS * WIDE // PIECE
-FORWARD = (0, 2, 4)
 RIM_X, RIM_B, RIM_C, K1, V1, KZ, K2, V2, KX, VX, K1S, V1S, E_B, T_SIB, T_C = range(15)
 E_A = 15
 E1 = E_A + CHUNKS
@@ -33,7 +33,7 @@
 IN = E2 + PIECES
 SQ = IN + CHUNKS
 COPIES = SQ + 3
-L_X, L_Z, L_Q, L_K, L_V, L_B, L_C, L_AO, L_MO = range(9)
+L_R, L_X, L_Z, L_Q, L_K, L_V, L_B, L_C, L_AO, L_SCALE, L_GATED = range(11)
 
 
 def dot(a, b):
@@ -77,9 +77,9 @@
     dt_bias,
     rates,
     skip_d,
-    gain,
     ao_hbm,
-    mo_hbm,
+    gated_hbm,
+    scale_hbm,
     xv,
     zv,
     qv,
@@ -88,6 +88,8 @@
     k_pass,
     bv,
     cv,
+    x_end,
+    x_ends,
     rim_x,
     rim_b,
     rim_c,
@@ -100,6 +102,8 @@
     e_n1,
     e_n2,
     e_pass,
+    e_pair,
+    chip_decay,
     in_own,
     in_sib,
     t_own,
@@ -119,7 +123,8 @@
     hot,
     tri_bias,
     ao,
-    mo,
+    gated_out,
+    scale_out,
     sumsq,
     send,
     recv,
@@ -160,7 +165,9 @@
             device_id_type=MESH,
         )
 
+    last_rows = pl.ds(TOK - 16, 16)
     loads = {
+        L_R: pltpu.make_async_copy(x_hbm.at[last_rows], x_end, local.at[L_R]),
         L_B: pltpu.make_async_copy(b_hbm, bv, local.at[L_B]),
         L_C: pltpu.make_async_copy(c_hbm, cv, local.at[L_C]),
         L_X: pltpu.make_async_copy(x_hbm, xv, local.at[L_X]),
@@ -177,15 +184,25 @@
         pl.semaphore_signal(
             barrier, inc=1, device_id=(p, lax.rem(t + n_tp - step, n_tp)), device_id_type=MESH
         )
-    for slot in (L_B, L_C, L_X, L_Z, L_K, L_V, L_Q):
+    for slot in (L_R, L_B, L_C, L_X, L_Z, L_K, L_V, L_Q):
         loads[slot].start()
+    loads[L_R].wait()
+    eighth = lax.broadcasted_iota(jnp.int32, (8, WIDE), 0)
+    for block in range(tiles // 4):
+        ends = [
+            x_end[:, (4 * block + i) * WIDE : (4 * block + i + 1) * WIDE].astype(F32)[8:]
+            for i in range(4)
+        ]
+        pairs = [
+            jnp.where(eighth < 4, pltpu.roll(ends[i], 4, 0), ends[i + 1]) for i in (0, 2)
+        ]
+        x_ends[block] = jnp.concatenate(pairs, axis=0).astype(BF16)
     pl.semaphore_wait(barrier, 5 + n_tp - 1)
 
-    last_rows = pl.ds(TOK - 16, 16)
     rims = [
         remote(b_hbm.at[last_rows], rim_b, RIM_B, at(1)),
         remote(c_hbm.at[last_rows], rim_c, RIM_C, at(1)),
-        remote(x_hbm.at[last_rows], rim_x, RIM_X, at(1)),
+        remote(x_ends, rim_x, RIM_X, at(1)),
     ]
     for copy in rims:
         copy.start()
@@ -270,12 +287,11 @@
         place = (lax.broadcasted_iota(jnp.int32, (128, WIDE), 1) >> 6) + tile * (WIDE // 64)
         return jnp.where(head == place, 1.0, 0.0).astype(BF16)
 
-    def conv(source, rim, weights, width):
+    def conv(source, rim8, weights, width):
         moved = dot(shift[...], source)
         taps = weights.astype(F32)
         total = taps[3:4] * source.astype(F32)
         edge = jnp.zeros((8, width), F32)
-        rim8 = rim.astype(F32)[8:16]
         for back in range(1, 4):
             tap = taps[3 - back : 4 - back]
             total = total + tap * moved[(back - 1) * TOK : back * TOK]
@@ -286,7 +302,7 @@
 
     loads[L_B].wait()
     rims[0].wait()
-    b_conv = conv(bv[...], rim_b[...], conv_b[...], bv.shape[1])
+    b_conv = conv(bv[...], rim_b[...].astype(F32)[8:], conv_b[...], bv.shape[1])
     for group in range(groups):
         b_group = b_conv[:, group * STATE : (group + 1) * STATE]
         ending = jnp.where(own_cols == last_id, b_group.astype(F32), 0.0)
@@ -302,14 +318,18 @@
     vectors = jnp.where(rows == 1, repeat_lanes(skip_d[...], 2), vectors)
     vectors = jnp.where(rows == 2, jnp.where(is_low, t_sib[0:1], 1.0), vectors)
     vectors = jnp.where(rows == 3, jnp.where(is_low, 1.0, t_own[0:1]), vectors)
+    vectors = jnp.where(rows == 4, t_chip[0:1], vectors)
     expand[pl.ds(2 * TOK, 16), :] = split2(vectors)
 
     loads[L_X].wait()
     rims[2].wait()
 
-    def end_state(tile):
+    def end_state(first, chunk):
+        tile = first + chunk
         here = pl.ds(pl.multiple_of(tile * WIDE, WIDE), WIDE)
-        x_conv = conv(xv[:, here], rim_x[:, here], conv_x[:, here], WIDE)
+        pair = rim_x[first // 4].astype(F32)[8 * (chunk // 2) : 8 * (chunk // 2) + 8]
+        rim8 = pltpu.roll(pair, 4, 0) if chunk % 2 == 0 else pair
+        x_conv = conv(xv[:, here], rim8, conv_x[:, here], WIDE)
         xv[:, here] = x_conv
         spread = spread_matrix(tile)
         factors = dot(expand[pl.ds(0, TOK), :], spread)
@@ -327,26 +347,33 @@
     halves = [
         remote(e_own.at[others + i], e_sib.at[others + i], E_A + i, sib) for i in range(CHUNKS)
     ]
-    nears = [remote(e_chip.at[i], e_n1.at[i], E1 + i, at(2)) for i in range(PIECES)]
-    downs = [
-        None if i in FORWARD else remote(e_chip.at[i], e_pass.at[i], EZ + i, lower)
-        for i in range(PIECES)
-    ]
-    passes = [
-        remote(e_n1.at[i], e_n2.at[i], E2 + i, at(2))
-        if i in FORWARD
-        else remote(e_pass.at[i], e_n2.at[i], E2 + i, pass_to)
-        for i in range(PIECES)
-    ]
+    odd = lax.rem(z_at, 2) == 1
+    firsts = [remote(e_chip.at[i], e_n1.at[i], E1 + i, at(2)) for i in range(PIECES)]
+    pairs = [remote(e_pair.at[i], e_n1.at[i], E1 + i, at(2)) for i in range(PIECES)]
+    downs = [remote(e_chip.at[i], e_pass.at[i], EZ + i, lower) for i in range(PIECES)]
+    passes = [remote(e_pass.at[i], e_n2.at[i], E2 + i, pass_to) for i in range(PIECES)]
 
     def pass_on(*pieces):
-        for i in pieces:
-            (nears[i] if i in FORWARD else downs[i]).wait_recv()
-            passes[i].start()
+        @pl.when(odd)
+        def _():
+            for i in pieces:
+                chunk, lane = divmod(i * PIECE, WIDE)
+                firsts[i].wait_recv()
+                e_pair[i] = (
+                    e_chip[i].astype(F32)
+                    + chip_decay[chunk, 4:5, lane : lane + PIECE] * e_n1[i].astype(F32)
+                ).astype(BF16)
+                pairs[i].start()
+
+        @pl.when(jnp.logical_not(odd))
+        def _():
+            for i in pieces:
+                downs[i].wait_recv()
+                passes[i].start()
 
     for step in range(CHUNKS + 1):
         if step < CHUNKS:
-            end_state(others + step)
+            end_state(others, step)
             halves[step].start()
         if step == 1:
             near[0].wait()
@@ -354,7 +381,8 @@
         if step == 0:
             continue
         chunk = step - 1
-        state, vectors = end_state(mine + chunk)
+        state, vectors = end_state(mine, chunk)
+        chip_decay[chunk] = vectors[:8]
         halves[chunk].wait()
         chip_end = (
             vectors[2:3] * state + vectors[3:4] * e_sib[mine + chunk].astype(F32)
@@ -362,9 +390,15 @@
         for i in range(WIDE // PIECE):
             piece = chunk * (WIDE // PIECE) + i
             e_chip[piece] = chip_end[:, i * PIECE : (i + 1) * PIECE]
-            nears[piece].start()
-            if downs[piece] is not None:
+
+            @pl.when(odd)
+            def _():
                 downs[piece].start()
+
+            @pl.when(jnp.logical_not(odd))
+            def _():
+                firsts[piece].start()
+
     half_b = remote(e_own.at[pl.ds(mine, CHUNKS)], e_sib.at[pl.ds(mine, CHUNKS)], E_B, sib)
     half_b.start()
     near[1].wait()
@@ -377,7 +411,7 @@
 
     loads[L_C].wait()
     rims[1].wait()
-    c_conv = conv(cv[...], rim_c[...], conv_c[...], cv.shape[1])
+    c_conv = conv(cv[...], rim_c[...].astype(F32)[8:], conv_c[...], cv.shape[1])
     for group in range(groups):
         b_group = b_conv[:, group * STATE : (group + 1) * STATE]
         c_group = c_conv[:, group * STATE : (group + 1) * STATE]
@@ -406,10 +440,8 @@
         gate[:, here] = leaving * open_gate
         return carry
 
-    lax.fori_loop(0, tiles // 2, gate_tile, 0, unroll=2)
+    lax.fori_loop(0, tiles, gate_tile, 0, unroll=2)
     pass_on(0, 1)
-    lax.fori_loop(tiles // 2, tiles, gate_tile, 0, unroll=2)
-    pass_on(2, 3)
 
     for copy in far:
         copy.wait()
@@ -437,19 +469,29 @@
     for slot in (L_K, L_V, L_Q):
         loads[slot].wait()
 
+    pass_on(2, 3)
+
     factor = HEAD_DIM**-0.5 * LOG2E
     query_heads = q_hbm.shape[1] // HEAD_DIM
     per_kv = query_heads // (k_hbm.shape[1] // HEAD_DIM)
 
-    def attend(head, carry):
+    def places(head):
         here = pl.ds(pl.multiple_of(head * HEAD_DIM, HEAD_DIM), HEAD_DIM)
         kv = pl.ds(pl.multiple_of((head // per_kv) * HEAD_DIM, HEAD_DIM), HEAD_DIM)
+        return here, kv
+
+    def score(head):
+        here, kv = places(head)
         query = jnp.concatenate([qv[:, here], far_own[...]], axis=1)
         scores = []
         for slot in range(5):
             key = jnp.concatenate([kbuf[slot, :, kv], hot[slot]], axis=1)
             scores.append(dot_nt(query, key))
         scores[0] = scores[0] + tri_bias[...]
+        return scores
+
+    def attend(head, scores):
+        here, kv = places(head)
         top = functools.reduce(jnp.maximum, scores)
         top = jnp.max(top, axis=1, keepdims=True) * factor
         ones = jnp.ones((TOK, HEAD_DIM), BF16)
@@ -459,7 +501,6 @@
             value = jnp.concatenate([vbuf[slot, :, kv], ones], axis=1)
             summed = summed + dot(weights, value)
         ao[:, here] = (summed[:, :HEAD_DIM] / summed[:, HEAD_DIM:]).astype(BF16)
-        return carry
 
     per_part = query_heads // CHUNKS
 
@@ -477,12 +518,18 @@
     lax.fori_loop(0, tiles, spread_tile, 0)
     sumsq[...] = jnp.zeros_like(sumsq)
 
+    def out_copy(tile, here):
+        return pltpu.make_async_copy(
+            gated_out.at[:, here], gated_hbm.at[:, here], local.at[L_GATED + tile]
+        )
+
     def join_tile(tile, incoming):
         here = pl.ds(pl.multiple_of(tile * WIDE, WIDE), WIDE)
         vectors = spread_in[tile]
         state = vectors[0:1] * e_sib[tile].astype(F32) + vectors[1:2] * incoming
         gated = g1[:, here] + gate[:, here] * dot(cj[tile // per_group], state.astype(BF16))
-        g1[:, here] = gated
+        gated_out[:, here] = gated.astype(BF16)
+        out_copy(tile, here).start()
         squares = gated * gated
         total = sumsq[...]
         for lane in range(WIDE // 128):
@@ -499,16 +546,23 @@
         for chunk in range(CHUNKS):
             tile = mine + chunk
             pieces = range(chunk * (WIDE // PIECE), (chunk + 1) * (WIDE // PIECE))
-            for i in pieces:
-                if i not in FORWARD:
-                    nears[i].wait_recv()
-                passes[i].wait_recv()
-            near_end = jnp.concatenate([e_n1[i] for i in pieces], axis=1).astype(F32)
-            far_end = jnp.concatenate([e_n2[i] for i in pieces], axis=1).astype(F32)
-            arriving = near_end + spread_in[tile][2:3] * far_end
-            in_own[chunk] = arriving.astype(BF16)
+
+            @pl.when(odd)
+            def _():
+                for i in pieces:
+                    passes[i].wait_recv()
+                near_end = jnp.concatenate([e_n1[i] for i in pieces], axis=1).astype(F32)
+                far_end = jnp.concatenate([e_n2[i] for i in pieces], axis=1).astype(F32)
+                in_own[chunk] = (near_end + spread_in[tile][2:3] * far_end).astype(BF16)
+
+            @pl.when(jnp.logical_not(odd))
+            def _():
+                for i in pieces:
+                    firsts[i].wait_recv()
+                in_own[chunk] = jnp.concatenate([e_n1[i] for i in pieces], axis=1)
+
             swaps[chunk].start()
-            join_tile(tile, arriving)
+            join_tile(tile, in_own[chunk].astype(F32))
         for chunk in range(CHUNKS):
             swaps[chunk].wait()
             join_tile(others + chunk, in_sib[chunk].astype(F32))
@@ -525,8 +579,13 @@
             copy.start()
 
     def attend_part(part, carry):
+        first = part * per_part
+        following = score(first)
         for i in range(per_part):
-            attend(part * per_part + i, carry)
+            scores = following
+            if i + 1 < per_part:
+                following = score(first + i + 1)
+            attend(first + i, scores)
 
         @pl.when(part == 0)
         def _():
@@ -547,11 +606,19 @@
     ao_out.start()
     for copy in sq_sends:
         copy.wait()
-    for i in range(PIECES):
-        nears[i].wait_send()
-        passes[i].wait_send()
-        if downs[i] is not None:
+
+    @pl.when(odd)
+    def _():
+        for i in range(PIECES):
             downs[i].wait_send()
+            pairs[i].wait_send()
+
+    @pl.when(jnp.logical_not(odd))
+    def _():
+        for i in range(PIECES):
+            firsts[i].wait_send()
+            passes[i].wait_send()
+
     total = sq_own[...]
     for step in range(1, n_tp):
         total = total + sq_in[step - 1]
@@ -563,22 +630,49 @@
         ],
         axis=0,
     )
-    scale_wide = repeat_lanes(scale_cols, WIDE // 128)
-
-    outs = []
+    scale_out[...] = scale_cols
+    scale_copy = pltpu.make_async_copy(scale_out, scale_hbm, local.at[L_SCALE])
+    scale_copy.start()
+    ao_out.wait()
     for tile in range(tiles):
-        here = slice(tile * WIDE, (tile + 1) * WIDE)
-        mo[:, here] = (g1[:, here] * scale_wide * gain[:, here]).astype(BF16)
-        out = pltpu.make_async_copy(
-            mo.at[:, pl.ds(tile * WIDE, WIDE)],
-            mo_hbm.at[:, pl.ds(tile * WIDE, WIDE)],
-            local.at[L_MO + tile],
-        )
-        out.start()
-        outs.append(out)
-    ao_out.wait()
-    for out in outs:
-        out.wait()
+        out_copy(tile, pl.ds(tile * WIDE, WIDE)).wait()
+    scale_copy.wait()
+
+
+def finish(ao_hbm, gated_hbm, scale_hbm, gain_hbm, ao_out, mo_out, ao, gated, scale, gain, mo, sems):
+    parts = PARTS
+    rows = TOK // parts
+    scale_in = pltpu.make_async_copy(scale_hbm, scale, sems.at[0])
+    gain_in = pltpu.make_async_copy(gain_hbm, gain, sems.at[1])
+    ao_in = pltpu.make_async_copy(ao_hbm, ao, sems.at[2])
+    ao_back = pltpu.make_async_copy(ao, ao_out, sems.at[3])
+
+    def part(i):
+        return pl.ds(i * rows, rows)
+
+    ins = [
+        pltpu.make_async_copy(gated_hbm.at[part(i)], gated.at[part(i)], sems.at[4 + i])
+        for i in range(parts)
+    ]
+    outs = [
+        pltpu.make_async_copy(mo.at[part(i)], mo_out.at[part(i)], sems.at[4 + parts + i])
+        for i in range(parts)
+    ]
+    for copy in [scale_in, gain_in, ins[0], ao_in] + ins[1:]:
+        copy.start()
+    scale_in.wait()
+    gain_in.wait()
+    for i in range(parts):
+        ins[i].wait()
+        wide = repeat_lanes(scale[part(i), :], gated.shape[1] // 128)
+        mo[part(i), :] = (gated[part(i), :].astype(F32) * wide * gain[...]).astype(BF16)
+        outs[i].start()
+        if i == 0:
+            ao_in.wait()
+            ao_back.start()
+    ao_back.wait()
+    for copy in outs:
+        copy.wait()
 
 
 def per_device(q, k, v, ids, x, b, c, z, dt_raw, conv_x, conv_b, conv_c, dt_bias, rates, skip_d, gain):
@@ -588,7 +682,7 @@
     groups = b.shape[1] // STATE
     hbm = pl.BlockSpec(memory_space=pl.ANY)
     vmem = pl.BlockSpec(memory_space=pltpu.VMEM)
-    specs = [hbm, hbm, hbm, vmem, hbm, hbm, hbm, hbm] + [vmem] * 8
+    specs = [hbm, hbm, hbm, vmem, hbm, hbm, hbm, hbm] + [vmem] * 7
     scratch = [
         pltpu.VMEM(x.shape, BF16),
         pltpu.VMEM(z.shape, BF16),
@@ -599,6 +693,8 @@
         pltpu.VMEM(b.shape, BF16),
         pltpu.VMEM(c.shape, BF16),
         pltpu.VMEM((16, channels), BF16),
+        pltpu.VMEM((tiles // 4, 16, WIDE), BF16),
+        pltpu.VMEM((tiles // 4, 16, WIDE), BF16),
         pltpu.VMEM((16, b.shape[1]), BF16),
         pltpu.VMEM((16, c.shape[1]), BF16),
         pltpu.VMEM(x.shape, BF16),
@@ -610,6 +706,8 @@
         pltpu.VMEM((PIECES, STATE, PIECE), BF16),
         pltpu.VMEM((PIECES, STATE, PIECE), BF16),
         pltpu.VMEM((PIECES, STATE, PIECE), BF16),
+        pltpu.VMEM((PIECES, STATE, PIECE), BF16),
+        pltpu.VMEM((CHUNKS, 8, WIDE), F32),
         pltpu.VMEM((CHUNKS, STATE, WIDE), BF16),
         pltpu.VMEM((CHUNKS, STATE, WIDE), BF16),
         pltpu.VMEM((8, 128), F32),
@@ -631,18 +729,20 @@
         pltpu.VMEM(q.shape, BF16),
         pltpu.VMEM(x.shape, BF16),
         pltpu.VMEM((TOK, 128), F32),
+        pltpu.VMEM((TOK, 128), F32),
         pltpu.SemaphoreType.DMA((COPIES,)),
         pltpu.SemaphoreType.DMA((COPIES,)),
-        pltpu.SemaphoreType.DMA((L_MO + tiles,)),
-    ]
-    return pl.pallas_call(
+        pltpu.SemaphoreType.DMA((L_GATED + tiles,)),
+    ]
+    ao, gated, scale = pl.pallas_call(
         functools.partial(kernel, n_ctx, n_tp),
         out_shape=(
             jax.ShapeDtypeStruct(q.shape, BF16),
             jax.ShapeDtypeStruct(x.shape, BF16),
+            jax.ShapeDtypeStruct((TOK, 128), F32),
         ),
         in_specs=specs,
-        out_specs=(hbm, hbm),
+        out_specs=(hbm, hbm, hbm),
         scratch_shapes=scratch,
         compiler_params=pltpu.CompilerParams(
             collective_id=1, has_side_effects=True, vmem_limit_bytes=56 * 2**20
@@ -664,8 +764,26 @@
         dt_bias[None],
         rates[None],
         skip_d[None],
-        gain[None],
     )
+    return pl.pallas_call(
+        finish,
+        out_shape=(
+            jax.ShapeDtypeStruct(q.shape, BF16),
+            jax.ShapeDtypeStruct(x.shape, BF16),
+        ),
+        in_specs=[hbm] * 4,
+        out_specs=(hbm, hbm),
+        scratch_shapes=[
+            pltpu.VMEM(q.shape, BF16),
+            pltpu.VMEM(x.shape, BF16),
+            pltpu.VMEM((TOK, 128), F32),
+            pltpu.VMEM((1, channels), F32),
+            pltpu.VMEM(x.shape, BF16),
+            pltpu.SemaphoreType.DMA((4 + 2 * PARTS,)),
+        ],
+        compiler_params=pltpu.CompilerParams(vmem_limit_bytes=60 * 2**20),
+        name="scale_rows",
+    )(ao, gated, scale, gain[None])
 
 
 def solution(mesh):

time: 49.5 us -> 47.6 us (0.962)
  local copies, waits for them, and re-layouts: 3.78 us -> 0 us
  Pallas kernels: 44.9 us -> 46.8 us
    unnamed x4 -> x0, local copies, waits for them, and re-layouts: 3.78 us -> none
    pallas_call x0 -> x1, Pallas kernels: none -> 3.07 us  [per_device(): pl.pallas_call(finish, out_shape=(jax.ShapeDtypeStruct(q.shape, BF16), ja...]
    pallas_call x1, Pallas kernels: 44.9 us -> 43.7 us  [per_device(): pl.pallas_call(functools.partial(kernel, n_ctx, n_tp), out_shape=(jax.Sha...]
where the time goes in v3:
time: 47.6 us; the launch traced here: 47.4 us
  Pallas kernels  46.8 us (98%)
  between operations  0.64 us (1%)
    pallas_call x1, Pallas kernels, per_device(): pl.pallas_call(functools.partial(kernel, n_ctx, n_tp), out_shape=(jax.Sha...  43.7 us
    pallas_call x1, Pallas kernels, per_device(): pl.pallas_call(finish, out_shape=(jax.ShapeDtypeStruct(q.shape, BF16), ja...  3.07 us

profile of v3, /device:TPU:1, one launch (start us, length us, event | category | flops | bytes accessed | tf_op | source)
XLA Modules:
  0.0 47.4 jit_solution(9104616272640809464)
XLA Ops:
  0.6 43.7 %packed_mix.1 = (bf16[256,2048]{1,0:T(8,128)(2,1)}, bf16[256,4096]{1,0:T(8,128)(2,1)}, f32[256,128]{1,0:T(8,128)}) custom-call(bf16[256,2048]{1,0:T(8,128)(2,1)} %q_hbm.1, bf16[256,256]{1,0:T(8,128)(2,1)} %k_hbm.1, bf16[256,256]{1,0:T(8,128)(2,1)} %v_hbm.1, s32[64,128]{1,0:T(8,128)} %bitcast.6, bf16[256,4096]{1,0:T(8,128)(2,1)} %x_hbm.1, ...), custom_call_target="tpu_custom_call" | custom-call | tf_op jit(solution)/shard_map/packed_mix/pallas_call | solution.py:737
  44.3 3.1 %scale_rows.1 = (bf16[256,2048]{1,0:T(8,128)(2,1)}, bf16[256,4096]{1,0:T(8,128)(2,1)}) custom-call(bf16[256,2048]{1,0:T(8,128)(2,1)} %get-tuple-element.5.ao_hbm, bf16[256,4096]{1,0:T(8,128)(2,1)} %get-tuple-element.6.gated_hbm, f32[256,128]{1,0:T(8,128)} %get-tuple-element.7.scale_hbm, f32[1,4096]{1,0:T(1,128)} %bitcast.8), custom_call_target="tpu_custom_call" | custom-call | tf_op jit(solution)/shard_map/scale_rows/pallas_call | solution.py:768

commit v4 on v3

--- a/solution.py
+++ b/solution.py
@@ -186,6 +186,16 @@
         )
     for slot in (L_R, L_B, L_C, L_X, L_Z, L_K, L_V, L_Q):
         loads[slot].start()
+    pl.semaphore_wait(barrier, 5 + n_tp - 1)
+
+    rims = [
+        remote(b_hbm.at[last_rows], rim_b, RIM_B, at(1)),
+        remote(c_hbm.at[last_rows], rim_c, RIM_C, at(1)),
+        remote(x_ends, rim_x, RIM_X, at(1)),
+    ]
+    k_down = remote(k_hbm, k_pass, KZ, lower)
+    for copy in (rims[0], rims[1], k_down):
+        copy.start()
     loads[L_R].wait()
     eighth = lax.broadcasted_iota(jnp.int32, (8, WIDE), 0)
     for block in range(tiles // 4):
@@ -197,27 +207,17 @@
             jnp.where(eighth < 4, pltpu.roll(ends[i], 4, 0), ends[i + 1]) for i in (0, 2)
         ]
         x_ends[block] = jnp.concatenate(pairs, axis=0).astype(BF16)
-    pl.semaphore_wait(barrier, 5 + n_tp - 1)
-
-    rims = [
-        remote(b_hbm.at[last_rows], rim_b, RIM_B, at(1)),
-        remote(c_hbm.at[last_rows], rim_c, RIM_C, at(1)),
-        remote(x_ends, rim_x, RIM_X, at(1)),
-    ]
-    for copy in rims:
-        copy.start()
+    rims[2].start()
     near = [
         remote(v_hbm, vbuf.at[1], V1, at(2)),
         remote(k_hbm, kbuf.at[1], K1, at(2)),
     ]
-    k_down = remote(k_hbm, k_pass, KZ, lower)
     far = [
         remote(vbuf.at[1], vbuf.at[3], V2, at(2)),
         remote(k_pass, kbuf.at[3], K2, pass_to),
     ]
     for copy in near:
         copy.start()
-    k_down.start()
     own_to_sib = [
         remote(k_hbm, kbuf.at[4], KX, sib),
         remote(v_hbm, vbuf.at[4], VX, sib),
@@ -375,10 +375,9 @@
         if step < CHUNKS:
             end_state(others, step)
             halves[step].start()
-        if step == 1:
+        if step == 0:
             near[0].wait()
             far[0].start()
-        if step == 0:
             continue
         chunk = step - 1
         state, vectors = end_state(mine, chunk)

time: 47.6 us -> 47.6 us (level)
  no operation moved by 1% of the time
where the time goes in v4:
time: 47.6 us; the launch traced here: 47.4 us
  Pallas kernels  46.7 us (98%)
  between operations  0.64 us (1%)
    pallas_call x1, Pallas kernels, per_device(): pl.pallas_call(functools.partial(kernel, n_ctx, n_tp), out_shape=(jax.Sha...  43.6 us
    pallas_call x1, Pallas kernels, per_device(): pl.pallas_call(finish, out_shape=(jax.ShapeDtypeStruct(q.shape, BF16), ja...  3.07 us

profile of v4, /device:TPU:1, one launch (start us, length us, event | category | flops | bytes accessed | tf_op | source)
XLA Modules:
  0.0 47.4 jit_solution(5696863828766129446)
XLA Ops:
  0.6 43.6 %packed_mix.1 = (bf16[256,2048]{1,0:T(8,128)(2,1)}, bf16[256,4096]{1,0:T(8,128)(2,1)}, f32[256,128]{1,0:T(8,128)}) custom-call(bf16[256,2048]{1,0:T(8,128)(2,1)} %q_hbm.1, bf16[256,256]{1,0:T(8,128)(2,1)} %k_hbm.1, bf16[256,256]{1,0:T(8,128)(2,1)} %v_hbm.1, s32[64,128]{1,0:T(8,128)} %bitcast.6, bf16[256,4096]{1,0:T(8,128)(2,1)} %x_hbm.1, ...), custom_call_target="tpu_custom_call" | custom-call | tf_op jit(solution)/shard_map/packed_mix/pallas_call | solution.py:736
  44.3 3.1 %scale_rows.1 = (bf16[256,2048]{1,0:T(8,128)(2,1)}, bf16[256,4096]{1,0:T(8,128)(2,1)}) custom-call(bf16[256,2048]{1,0:T(8,128)(2,1)} %get-tuple-element.5.ao_hbm, bf16[256,4096]{1,0:T(8,128)(2,1)} %get-tuple-element.6.gated_hbm, f32[256,128]{1,0:T(8,128)} %get-tuple-element.7.scale_hbm, f32[1,4096]{1,0:T(1,128)} %bitcast.8), custom_call_target="tpu_custom_call" | custom-call | tf_op jit(solution)/shard_map/scale_rows/pallas_call | solution.py:767
